TPU v7x, 256 devices: a whole 4x4x8 slice. The times are simulated.
256 devices in a mesh: dp: 8 (over y, core), tensor: 32 (over x, z).
Axes of the slice: x: 4, y: 4, z: 8, core: 2. Of those that a mesh axis runs over, the one named last changes fastest.
Arguments:
- grad: bfloat16 [8, 3584, 9472], P('dp', 'tensor'), may hold values from -70 to 70
- error: float32 [8, 3584, 9472], P('dp', 'tensor'), may hold values from -3 to 3
- q_init: float32 [8, 9472], replicated, may hold values from -4 to 4
Outputs:
- decompressed: bfloat16 [3584, 9472], P('tensor')
- new_error: float32 [8, 3584, 9472], P('dp', 'tensor')
- q_next: float32 [8, 9472], replicated
All inputs are finite; a program needn't handle non-finite values.
Results may differ from a plain program's by a relative error of at most 0.0025.
Values sent between devices are 32-bit elements; how exact they have to be, the bound alone decides.
A program may use at most 64 MiB of HBM per device.

v0:
```python
import jax
import jax.numpy as jnp
from jax import lax
from jax.sharding import PartitionSpec as P

ITERS = 4


highest = lax.Precision.HIGHEST


def solve_lower(factor, block):
    return lax.linalg.triangular_solve(factor, block, left_side=True, lower=True)


def gram_factor(p_sum):
    local_gram = jnp.dot(p_sum, p_sum.T, precision=highest)
    gram_total = lax.psum(local_gram, "tensor")
    return jnp.linalg.cholesky(gram_total)


def reduce_columns(q_term):
    return lax.psum(q_term, ("dp", "tensor"))


def local(grad, error, q_init):
    replicas = lax.axis_size("dp")
    merged = grad[0].astype(jnp.float32) + error[0]
    q_hat = q_init
    for iteration in range(ITERS):
        p_term = jnp.einsum("kc,rc->kr", q_hat, merged, precision=highest)
        p_sum = lax.psum(p_term, "dp") / replicas
        factor = gram_factor(p_sum)
        p_hat = solve_lower(factor, p_sum)
        q_term = jnp.einsum("kr,rc->kc", p_hat, merged, precision=highest)
        q_sum = reduce_columns(q_term) / replicas
        q_hat = q_sum
    approx = jnp.dot(p_hat.T, q_sum, precision=highest)
    return (approx.astype(jnp.bfloat16), (merged - approx)[None], q_sum)


def solution(mesh):
    return jax.shard_map(
        local,
        mesh=mesh,
        in_specs=(P("dp", "tensor", None), P("dp", "tensor", None), P()),
        out_specs=(P("tensor", None), P("dp", "tensor", None), P()),
        check_vma=False,
    )
```

profile of v0, /device:TPU:1, one launch (start us, length us, event | category | flops | bytes accessed | tf_op | source)
XLA Modules:
  0.0 1374.8 jit_solution(1752435451764602820)
XLA Ops:
  7.2 3.3 convert_add_fusion
  10.5 2.0 copy-done.1
  12.5 3.4 fusion.17
  15.9 15.0 %psum.84 = f32[8,112]{1,0:T(8,128)S(1)} all-reduce(f32[8,112]{1,0:T(8,128)S(1)} %fusion.17), channel_id=1, replica_groups=mesh['dp'=8,'tensor'=32] {'dp'}, use_global_device_ids=true, to_apply=%region_0.0 | all-reduce | flops 896 | bytes 7168 | tf_op jit(solution)/shard_map/psum | solution.py:32
  31.0 61.9 %psum.85 = f32[8,8]{0,1:T(8,128)S(1)} all-reduce(f32[8,8]{0,1:T(8,128)S(1)} %fusion.58), channel_id=1, replica_groups=mesh['dp'=8,'tensor'=32] {'tensor'}, use_global_device_ids=true, to_apply=%region_1.0 | all-reduce | flops 64 | bytes 512 | tf_op jit(solution)/shard_map/psum | solution.py:18
  95.9 5.0 fusion.12
  101.0 252.0 %all-reduce.5.cloned.1.call-done = f32[8,9472]{1,0:T(8,128)} async-done(((f32[8,9472]{1,0:T(8,128)}), f32[8,9472]{1,0:T(8,128)}) %all-reduce.5.cloned.1.call-update) | async-done | bytes 303120 | tf_op jit(solution)/shard_map/psum | solution.py:23
  353.0 5.7 fusion.10
  358.6 12.3 psum.87
  371.1 57.1 %psum.88 = f32[8,8]{0,1:T(8,128)S(1)} all-reduce(f32[8,8]{0,1:T(8,128)S(1)} %fusion.55), channel_id=1, replica_groups=mesh['dp'=8,'tensor'=32] {'tensor'}, use_global_device_ids=true, to_apply=%region_6.9 | all-reduce | flops 64 | bytes 512 | tf_op jit(solution)/shard_map/psum | solution.py:18
  431.1 5.0 fusion.8
  436.4 252.2 %all-reduce.7.cloned.1.call-done = f32[8,9472]{1,0:T(8,128)} async-done(((f32[8,9472]{1,0:T(8,128)}), f32[8,9472]{1,0:T(8,128)}) %all-reduce.7.cloned.1.call-update) | async-done | bytes 303120 | tf_op jit(solution)/shard_map/psum | solution.py:23
  688.6 5.7 fusion.6
  694.3 12.3 psum.90
  706.7 57.1 %psum.91 = f32[8,8]{0,1:T(8,128)S(1)} all-reduce(f32[8,8]{0,1:T(8,128)S(1)} %fusion.52), channel_id=1, replica_groups=mesh['dp'=8,'tensor'=32] {'tensor'}, use_global_device_ids=true, to_apply=%region_9.12 | all-reduce | flops 64 | bytes 512 | tf_op jit(solution)/shard_map/psum | solution.py:18
  766.8 5.0 fusion.4
  771.9 252.4 %all-reduce.9.cloned.1.call-done = f32[8,9472]{1,0:T(8,128)} async-done(((f32[8,9472]{1,0:T(8,128)}), f32[8,9472]{1,0:T(8,128)}) %all-reduce.9.cloned.1.call-update) | async-done | bytes 303120 | tf_op jit(solution)/shard_map/psum | solution.py:23
  1024.3 5.7 fusion.2
  1030.0 12.3 psum.93
  1042.4 57.3 %psum.94 = f32[8,8]{0,1:T(8,128)S(1)} all-reduce(f32[8,8]{0,1:T(8,128)S(1)} %fusion.49), channel_id=1, replica_groups=mesh['dp'=8,'tensor'=32] {'tensor'}, use_global_device_ids=true, to_apply=%region_12.15 | all-reduce | flops 64 | bytes 512 | tf_op jit(solution)/shard_map/psum | solution.py:18
  1102.6 5.0 fusion
  1107.7 252.5 %all-reduce.11.cloned.1.call-done = f32[8,9472]{1,0:T(8,128)} async-done(((f32[8,9472]{1,0:T(8,128)}), f32[8,9472]{1,0:T(8,128)}) %all-reduce.11.cloned.1.call-update) | async-done | bytes 303120 | tf_op jit(solution)/shard_map/psum | solution.py:23
  1360.1 1.0 broadcast_multiply_fusion
  1361.1 7.1 fusion.16
  (49 shorter events, 12.7 us)
Async XLA Ops:
  7.2 5.4 copy-start
  7.2 345.8 %all-reduce.5.cloned.1.call-start = ((), (), s32[]{:S(2)}) async-start(), calls=%async_computation | async-start | bytes 606208 | tf_op jit(solution)/shard_map/psum | solution.py:23
  10.5 2.0 copy-start.1
  101.0 587.7 %all-reduce.7.cloned.1.call-start = ((), (), s32[]{:S(2)}) async-start(), calls=%async_computation.1 | async-start | bytes 606208 | tf_op jit(solution)/shard_map/psum | solution.py:23
  436.1 588.1 %all-reduce.9.cloned.1.call-start = ((), (), s32[]{:S(2)}) async-start(), calls=%async_computation.2 | async-start | bytes 606208 | tf_op jit(solution)/shard_map/psum | solution.py:23
  771.8 588.3 %all-reduce.11.cloned.1.call-start = ((), (), s32[]{:S(2)}) async-start(), calls=%async_computation.3 | async-start | bytes 606208 | tf_op jit(solution)/shard_map/psum | solution.py:23
  1361.1 7.1 copy-start.2
Sparse Core Ops, SparseCore 0:
  101.1 251.8 all-reduce.4
  436.3 252.3 all-reduce.6
  771.9 252.3 all-reduce.8
  1107.8 252.3 all-reduce.10
where the time goes:
time: 1380 us; the launch traced here: 1370 us
  waiting for transfers between devices  1010 us (73%)
  blocking collectives  285 us (21%)
  matrix products  48.9 us (4%)
  other arithmetic  14.9 us (1%)
  between operations  13.9 us (1%)
    psum x4, waiting for transfers between devices, reduce_columns(): return lax.psum(q_term, ('dp', 'tensor'))  1010 us
    psum x4, blocking collectives, gram_factor(): gram_total = lax.psum(local_gram, 'tensor')  233 us
    psum x4, blocking collectives, local(): p_sum = lax.psum(p_term, 'dp') / replicas  52 us
  transfers between devices with their start and end apart: 4, of which 4 were waited for; matrix products, arithmetic and copies ran while one was open for 0% of the time, Pallas kernels for 0%

commit v1 on v0

v1 whole, which is shorter than its diff:
```python
import jax
import jax.numpy as jnp
from jax import lax
from jax.experimental import pallas as pl
from jax.experimental.pallas import tpu as pltpu
from jax.sharding import PartitionSpec as P

MESH = pl.DeviceIdType.MESH
F32, BF16 = jnp.float32, jnp.bfloat16
ITERS = 4
RANK = 8
ROWS = 112
HALF = 56
COLS = 9472
LANE = 128
WIN = 640
STEP_Y = 18 * LANE
TOP = 32
PART = 24
CHUNK = 10 * LANE
STARTS = tuple(range(0, COLS, CHUNK))


def nt(a, b):
    return lax.dot_general(a, b, (((1,), (1,)), ((), ())), preferred_element_type=F32)


def nn(a, b):
    return lax.dot_general(a, b, (((1,), (0,)), ((), ())), preferred_element_type=F32)


def two_terms(a):
    high = a.astype(BF16).astype(F32)
    return high, a - high


def stacked(a):
    return jnp.concatenate(two_terms(a), axis=0).astype(BF16)


def inverse_factor(gram):
    shape = (RANK, LANE)
    row = lax.broadcasted_iota(jnp.int32, shape, 0)
    lane = lax.broadcasted_iota(jnp.int32, shape, 1)
    work = jnp.where(lane == row + RANK, 1.0, jnp.where(lane < RANK, gram, 0.0))
    for j in range(RANK - 1):
        scale = work[:, j : j + 1] / work[j : j + 1, j : j + 1]
        work = work - jnp.where(row > j, scale * work[j : j + 1, :], 0.0)
    diagonal = jnp.sum(jnp.where(lane == row, work, 0.0), axis=1, keepdims=True)
    return work[:, RANK : 2 * RANK] / jnp.sqrt(diagonal)


def apply(inverse, block):
    total = inverse[:, 0:1] * block[0:1, :]
    for j in range(1, RANK):
        total = total + inverse[:, j : j + 1] * block[j : j + 1, :]
    return total


def by_column(low, high):
    tiles = [
        jnp.concatenate([low[4 * i : 4 * i + 4], high[4 * i : 4 * i + 4]], axis=0)
        for i in range(6)
    ]
    return jnp.concatenate(tiles[:5], axis=1), tiles[5]


def power(
    grad, error, q_init, q_out, p_out,
    gbuf, m, qv, cr, ra, rb, fm, fp, sx, s, s_high, s_low,
    p1s, p1r, qs, cbuf, zs, zbuf, qall, ps, pbuf, pfin, qfin,
    lsem, csend, crecv, ysend, yrecv, xsem, p1sem, c1sem, zsem, c2sem, psem, fsem,
):
    d, t = lax.axis_index("dp"), lax.axis_index("tensor")
    y, c = d // 2, d % 2
    x, z = t // 8, t % 8

    def at(y_, c_, x_, z_):
        return (y_ * 2 + c_, x_ * 8 + z_)

    other = at(y, 1 - c, x, z)
    ahead_y, behind_y, far_y = (y + 1 + 2 * c) % 4, (y + 3 - 2 * c) % 4, (y + 2) % 4
    ahead, behind = at(ahead_y, c, x, z), at(behind_y, c, x, z)
    plane = [((y + j) % 4, (x + i) % 4) for i in range(4) for j in range(4)]
    plane_same = [at(yy, c, xx, z) for yy, xx in plane[1:]]
    plane_other = [at(yy, 1 - c, xx, z) for yy, xx in plane[1:]]
    line = [at(y, c, x, (z + k) % 8) for k in range(1, 8)]

    def remote(src, dst, send, recv, device):
        copy = pltpu.make_async_remote_copy(
            src, dst, send, recv, device_id=device, device_id_type=MESH
        )
        copy.start()

    def wait(ref, sem):
        pltpu.make_async_copy(ref, ref, sem).wait()

    barrier = pltpu.get_barrier_semaphore()
    partners = [other] + plane_same + plane_other + line
    for device in partners:
        pl.semaphore_signal(barrier, inc=1, device_id=device, device_id_type=MESH)

    n = len(STARTS)
    loads = []
    for i, start in enumerate(STARTS):
        columns = pl.ds(start, min(CHUNK, COLS - start))
        loads.append((
            pltpu.make_async_copy(grad.at[0, :, columns], gbuf.at[:, columns], lsem.at[i]),
            pltpu.make_async_copy(error.at[0, :, columns], m.at[:, columns], lsem.at[n + i]),
        ))
        for copy in loads[-1]:
            copy.start()
    q_load = pltpu.make_async_copy(q_init, qv, lsem.at[2 * n])
    q_load.start()
    for i, start in enumerate(STARTS):
        for copy in loads[i]:
            copy.wait()
        columns = pl.ds(start, min(CHUNK, COLS - start))
        m[:, columns] = gbuf[:, columns].astype(F32) + m[:, columns]
    q_load.wait()
    pl.semaphore_wait(barrier, len(partners))

    def window(yy, xx):
        return pl.ds(pl.multiple_of(yy * STEP_Y + xx * WIN, LANE), WIN)

    mine = pl.ds(pl.multiple_of(HALF * c, 8), HALF)
    theirs = pl.ds(pl.multiple_of(HALF * (1 - c), 8), HALF)
    order = [(x + 1 + j) % 4 for j in range(4)]
    for j in range(4):
        for yy in range(4):
            remote(m.at[theirs, window(yy, order[j])], cr.at[order[j], yy], csend.at[j], crecv.at[j], other)

    top, low = pl.ds(0, TOP), pl.ds(TOP, HALF - TOP)

    def first(j):
        xx = order[j]
        wait(cr.at[xx], crecv.at[j])
        cr[xx, far_y] = cr[xx, far_y] + m[mine, window(far_y, xx)]
        remote(cr.at[xx, far_y, top], ra.at[j], ysend.at[0, j], yrecv.at[0, j], ahead)
        remote(cr.at[xx, far_y, low], rb.at[j], ysend.at[1, j], yrecv.at[1, j], behind)
        cr[xx, ahead_y] = cr[xx, ahead_y] + m[mine, window(ahead_y, xx)]
        remote(cr.at[xx, ahead_y, low], fm.at[j, low], ysend.at[2, j], yrecv.at[2, j], ahead)
        cr[xx, behind_y] = cr[xx, behind_y] + m[mine, window(behind_y, xx)]
        remote(cr.at[xx, behind_y, top], fp.at[j, top], ysend.at[3, j], yrecv.at[3, j], behind)
        cr[xx, y] = cr[xx, y] + m[mine, window(y, xx)]

    def second(j):
        xx = order[j]
        wait(ra.at[j], yrecv.at[0, j])
        ra[j] = ra[j] + cr[xx, ahead_y, top]
        remote(ra.at[j], fm.at[j, top], ysend.at[4, j], yrecv.at[4, j], ahead)
        wait(rb.at[j], yrecv.at[1, j])
        rb[j] = rb[j] + cr[xx, behind_y, low]
        remote(rb.at[j], fp.at[j, low], ysend.at[5, j], yrecv.at[5, j], behind)

    here = pl.ds(pl.multiple_of(HALF * x, 8), HALF)

    def third(j):
        xx = order[j]
        wait(fm.at[j, low], yrecv.at[2, j])
        wait(fp.at[j, top], yrecv.at[3, j])
        wait(fm.at[j, top], yrecv.at[4, j])
        wait(fp.at[j, low], yrecv.at[5, j])
        total = (fm[j] + fp[j] + cr[xx, y]) * 0.125
        if j < 3:
            sx[j] = total
            remote(sx.at[j], s.at[here], xsem.at[0], xsem.at[1], at(y, c, xx, z))
        else:
            s[here] = total

    first(0)

    q_two = stacked(qv[...])
    p_term = jnp.zeros((RANK, ROWS), F32)
    for start in STARTS:
        stop = min(start + CHUNK, COLS)
        high, rest = two_terms(m[:, start:stop])
        q_part = q_two[:, start:stop]
        on_high = nt(q_part, high.astype(BF16))
        on_rest = nt(q_part, rest.astype(BF16))
        p_term = p_term + (on_high[:RANK] + on_high[RANK:]) + (on_rest[:RANK] + on_rest[RANK:])
    blank = jnp.zeros((RANK, LANE - HALF), F32)
    for half in range(2):
        p1s[half] = jnp.concatenate([p_term[:, HALF * half : HALF * half + HALF], blank], axis=1)
    place = x * 8 + d
    p1r[place] = p1s[c]
    for same, cross in zip(plane_same, plane_other):
        remote(p1s.at[c], p1r.at[place], p1sem.at[0], p1sem.at[1], same)
        remote(p1s.at[1 - c], p1r.at[place], p1sem.at[0], p1sem.at[1], cross)
    remote(p1s.at[1 - c], p1r.at[place], p1sem.at[0], p1sem.at[1], other)

    first(1)
    second(0)
    first(2)
    second(1)
    third(0)
    first(3)
    second(2)
    third(1)
    second(3)
    third(2)
    third(3)

    wait(p1r.at[pl.ds(0, 31)], p1sem.at[1])
    blocks = []
    for xx in range(4):
        total = p1r[8 * xx]
        for dd in range(1, 8):
            total = total + p1r[8 * xx + dd]
        blocks.append(total[:, :HALF])
    p_sum = jnp.concatenate(blocks, axis=1) * 0.125

    wait(s.at[pl.ds(0, 3 * HALF)], xsem.at[1])
    limit = jnp.where(jnp.logical_and(x == 3, y < 3), 3 * LANE, WIN)
    inside = lax.broadcasted_iota(jnp.int32, (4 * HALF, WIN), 1) < limit
    high, rest = two_terms(jnp.where(inside, s[...], 0.0))
    s_high[...] = high.astype(BF16)
    s_low[...] = rest.astype(BF16)

    own = pl.ds(pl.multiple_of(PART * c, 8), PART)
    cross = pl.ds(pl.multiple_of(PART * (1 - c), 8), PART)
    pad = jnp.zeros((RANK, LANE - RANK), F32)
    me = y * 4 + x
    for i in range(ITERS):
        last = i == ITERS - 1
        p_two = stacked(p_sum)
        a, b = nn(p_two, s_high[...]), nn(p_two, s_low[...])
        q_raw = (a[:RANK] + a[RANK:]) + (b[:RANK] + b[RANK:])
        gram = lax.dot_general(
            p_sum, p_sum, (((1,), (1,)), ((), ())),
            precision=lax.Precision.HIGHEST, preferred_element_type=F32,
        )
        gram = jnp.concatenate([gram, pad], axis=1)
        for half in range(2):
            ranks = slice(4 * half, 4 * half + 4)
            for k in range(5):
                qs[i, PART * half + 4 * k : PART * half + 4 * k + 4, :] = q_raw[ranks, LANE * k : LANE * k + LANE]
            qs[i, PART * half + 20 : PART * half + 24, :] = gram[ranks]
        remote(qs.at[i, cross], cbuf.at[i], c1sem.at[0, i], c1sem.at[1, i], other)
        if last:
            rows = jnp.zeros((RANK, HALF), F32)
            for xx in range(4):
                rows = jnp.where(x == xx, p_sum[:, HALF * xx : HALF * xx + HALF], rows)
            pfin[c] = jnp.concatenate([rows, blank], axis=1)
            remote(pfin.at[c], pfin.at[c], fsem.at[0], fsem.at[1], other)
        wait(cbuf.at[i], c1sem.at[1, i])
        zs[i] = qs[i, own] + cbuf[i]
        zbuf[i, z] = zs[i]
        for device in line:
            remote(zs.at[i], zbuf.at[i, z], zsem.at[0, i], zsem.at[1, i], device)
        wait(zbuf.at[i, pl.ds(0, 7)], zsem.at[1, i])
        total = zbuf[i, 0]
        for k in range(1, 8):
            total = total + zbuf[i, k]
        if last:
            break
        qall[i, own] = total
        remote(qall.at[i, own], qall.at[i, own], c2sem.at[0, i], c2sem.at[1, i], other)
        wait(qall.at[i, own], c2sem.at[1, i])
        q_raw, gram = by_column(qall[i, 0:PART, :], qall[i, PART : 2 * PART, :])
        q_two = stacked(q_raw)
        a, b = nt(q_two, s_high[...]), nt(q_two, s_low[...])
        p_raw = (a[:RANK] + a[RANK:]) + (b[:RANK] + b[RANK:])
        ps[i, 0:RANK, :] = p_raw[:, :LANE]
        ps[i, RANK : 2 * RANK, :] = jnp.concatenate(
            [p_raw[:, LANE:], jnp.zeros((RANK, 2 * LANE - 4 * HALF), F32)], axis=1
        )
        for device in plane_same:
            remote(ps.at[i], pbuf.at[i, me], psem.at[0, i], psem.at[1, i], device)
        pbuf[i, me] = ps[i]
        inverse = inverse_factor(gram)
        wait(pbuf.at[i, pl.ds(0, 15)], psem.at[1, i])
        p_raw = pbuf[i, 0]
        for k in range(1, 16):
            p_raw = p_raw + pbuf[i, k]
        p_raw = jnp.concatenate([p_raw[:RANK], p_raw[RANK:, : 4 * HALF - LANE]], axis=1)
        p_sum = apply(inverse, p_raw)

    slot = me * 2 + c
    qfin[slot] = total
    remote(qfin.at[slot], qfin.at[slot], fsem.at[2], fsem.at[3], other)
    for same, cross in zip(plane_same, plane_other):
        remote(qfin.at[slot], qfin.at[slot], fsem.at[4], fsem.at[5], same)
        remote(qfin.at[slot], qfin.at[slot], fsem.at[4], fsem.at[5], cross)
    wait(qfin.at[slot], fsem.at[3])
    wait(pfin.at[c], fsem.at[1])
    _, gram = by_column(qfin[me * 2], qfin[me * 2 + 1])
    inverse = inverse_factor(gram)
    p_hat = apply(inverse, jnp.concatenate([pfin[0][:, :HALF], pfin[1][:, :HALF]], axis=1))
    p_out[...] = jnp.concatenate([p_hat, jnp.zeros((RANK, LANE - ROWS), F32)], axis=1)
    wait(qfin.at[pl.ds(0, 30)], fsem.at[5])
    for yy in range(4):
        for xx in range(4):
            group = (yy * 4 + xx) * 2
            q_raw, _ = by_column(qfin[group], qfin[group + 1])
            width = 3 * LANE if xx == 3 and yy < 3 else WIN
            start = yy * STEP_Y + xx * WIN
            q_out[:, start : start + width] = apply(inverse, q_raw[:, :width])

    for j in range(4):
        wait(cr.at[j], csend.at[j])
        wait(ra.at[j], ysend.at[0, j])
        wait(rb.at[j], ysend.at[1, j])
        wait(fm.at[j, low], ysend.at[2, j])
        wait(fp.at[j, top], ysend.at[3, j])
        wait(ra.at[j], ysend.at[4, j])
        wait(rb.at[j], ysend.at[5, j])
    wait(sx, xsem.at[0])
    wait(p1r.at[pl.ds(0, 31)], p1sem.at[0])
    for i in range(ITERS):
        wait(cbuf.at[i], c1sem.at[0, i])
        wait(zbuf.at[i, pl.ds(0, 7)], zsem.at[0, i])
        if i < ITERS - 1:
            wait(cbuf.at[i], c2sem.at[0, i])
            wait(pbuf.at[i, pl.ds(0, 15)], psem.at[0, i])
    wait(pfin.at[0], fsem.at[0])
    wait(cbuf.at[0], fsem.at[2])
    wait(qfin.at[pl.ds(0, 30)], fsem.at[4])


def factors(grad, error, q_init):
    dma = pltpu.SemaphoreType.DMA
    vmem = pltpu.VMEM
    return pl.pallas_call(
        power,
        name="factors",
        out_shape=(
            jax.ShapeDtypeStruct((RANK, COLS), F32),
            jax.ShapeDtypeStruct((RANK, LANE), F32),
        ),
        in_specs=[pl.BlockSpec(memory_space=pl.ANY)] * 3,
        out_specs=(pl.BlockSpec(memory_space=vmem), pl.BlockSpec(memory_space=vmem)),
        scratch_shapes=[
            vmem((ROWS, COLS), BF16),
            vmem((ROWS, COLS), F32),
            vmem((RANK, COLS), F32),
            vmem((4, 4, HALF, WIN), F32),
            vmem((4, TOP, WIN), F32),
            vmem((4, HALF - TOP, WIN), F32),
            vmem((4, HALF, WIN), F32),
            vmem((4, HALF, WIN), F32),
            vmem((3, HALF, WIN), F32),
            vmem((4 * HALF, WIN), F32),
            vmem((4 * HALF, WIN), BF16),
            vmem((4 * HALF, WIN), BF16),
            vmem((2, RANK, LANE), F32),
            vmem((32, RANK, LANE), F32),
            vmem((ITERS, 2 * PART, LANE), F32),
            vmem((ITERS, PART, LANE), F32),
            vmem((ITERS, PART, LANE), F32),
            vmem((ITERS, 8, PART, LANE), F32),
            vmem((ITERS, 2 * PART, LANE), F32),
            vmem((ITERS, 2 * RANK, LANE), F32),
            vmem((ITERS, 16, 2 * RANK, LANE), F32),
            vmem((2, RANK, LANE), F32),
            vmem((32, PART, LANE), F32),
            dma((2 * len(STARTS) + 1,)),
            dma((4,)),
            dma((4,)),
            dma((6, 4)),
            dma((6, 4)),
            dma((2,)),
            dma((2,)),
            dma((2, ITERS)),
            dma((2, ITERS)),
            dma((2, ITERS)),
            dma((2, ITERS)),
            dma((6,)),
        ],
        compiler_params=pltpu.CompilerParams(
            collective_id=0, has_side_effects=True, vmem_limit_bytes=40 * 2**20
        ),
    )(grad, error, q_init)


def finish(p, q, grad, error, decompressed, new_error, q_next):
    p_high, p_rest = two_terms(p[:, :ROWS])
    q_high, q_rest = two_terms(q[...])
    left = jnp.concatenate([p_high, p_high, p_rest, p_rest], axis=0).astype(BF16)
    right = jnp.concatenate([q_high, q_rest, q_high, q_rest], axis=0).astype(BF16)
    approx = lax.dot_general(
        left, right, (((0,), (0,)), ((), ())), preferred_element_type=F32
    )
    decompressed[...] = approx.astype(BF16)
    new_error[...] = (grad[...].astype(F32) + error[...]) - approx
    q_next[...] = q[...]


def outputs(p_hat, q_sum, grad, error):
    def block(rows):
        return pl.BlockSpec((rows, CHUNK), lambda i: (0, i))

    whole = pl.BlockSpec((None, ROWS, CHUNK), lambda i: (0, 0, i))
    return pl.pallas_call(
        finish,
        name="outputs",
        grid=(len(STARTS),),
        in_specs=[pl.BlockSpec((RANK, LANE), lambda i: (0, 0)), block(RANK), whole, whole],
        out_specs=(block(ROWS), whole, block(RANK)),
        out_shape=(
            jax.ShapeDtypeStruct((ROWS, COLS), BF16),
            jax.ShapeDtypeStruct((1, ROWS, COLS), F32),
            jax.ShapeDtypeStruct((RANK, COLS), F32),
        ),
        compiler_params=pltpu.CompilerParams(vmem_limit_bytes=24 * 2**20),
    )(p_hat, q_sum, grad, error)


def local(grad, error, q_init):
    q_sum, p_hat = factors(grad, error, q_init)
    return outputs(p_hat, q_sum, grad, error)


def solution(mesh):
    return jax.shard_map(
        local,
        mesh=mesh,
        in_specs=(P("dp", "tensor", None), P("dp", "tensor", None), P()),
        out_specs=(P("tensor", None), P("dp", "tensor", None), P()),
        check_vma=False,
    )
```

time: 1380 us -> 103 us (0.07)
  waiting for transfers between devices: 1010 us -> 0 us
  blocking collectives: 285 us -> 0 us
  Pallas kernels: 0 us -> 97.8 us
  matrix products: 48.9 us -> 0 us
  other arithmetic: 14.9 us -> 0 us
    psum x4 -> x0, waiting for transfers between devices: 1010 us -> none  [reduce_columns(): return lax.psum(q_term, ('dp', 'tensor'))]
    psum x8 -> x0, blocking collectives: 285 us -> none  [the longest x4 233 us: gram_factor(): gram_total = lax.psum(local_gram, 'tensor')]
    pallas_call x0 -> x2, Pallas kernels: none -> 97.8 us  [the longest x1 92.4 us: factors(): pl.pallas_call(power, name='factors', out_shape=(jax.ShapeDtypeStruct((RA...]
    dot_general x13 -> x0, matrix products: 48.1 us -> none  [the longest x4 20.4 us: local(): p_term = jnp.einsum('kc,rc->kr', q_hat, merged, precision=highest)]
  transfers between devices with their start and end apart: 4 -> 0, of which waited for: 4 -> 0; matrix products, arithmetic and copies ran while one was open for 0% -> 0% of each run, Pallas kernels for 0% -> 0%
where the time goes in v1:
time: 103 us
  Pallas kernels  97.8 us (95%)
  local copies, waits for them, and re-layouts  4.76 us (5%)
    pallas_call x1, Pallas kernels, factors(): pl.pallas_call(power, name='factors', out_shape=(jax.ShapeDtypeStruct((RA...  92.4 us
    pallas_call x1, Pallas kernels, outputs(): pl.pallas_call(finish, name='outputs', grid=(len(STARTS),), in_specs=[pl....  5.39 us
    unnamed x6, local copies, waits for them, and re-layouts  4.76 us

profile of v1, /device:TPU:1, one launch (start us, length us, event | category | flops | bytes accessed | tf_op | source)
XLA Modules:
  0.0 103.2 jit_solution(6310850506676125283)
XLA Ops:
  0.6 0.0 copy-start
  0.6 2.2 %copy-done = f32[1,112,9472]{2,1,0:T(8,128)S(1)} copy-done((f32[1,112,9472]{2,1,0:T(8,128)S(1)}, f32[1,112,9472]{2,1,0:T(8,128)}, u32[]{:S(2)}) %copy-start) | copy-done | bytes 4243480
  2.8 0.0 copy-start.1
  2.8 1.6 %copy-done.1 = bf16[1,112,9472]{2,1,0:T(8,128)(2,1)S(1)} copy-done((bf16[1,112,9472]{2,1,0:T(8,128)(2,1)S(1)}, bf16[1,112,9472]{2,1,0:T(8,128)(2,1)}, u32[]{:S(2)}) %copy-start.1) | copy-done | bytes 2121752
  4.4 0.0 copy-start.2
  4.4 1.0 copy-done.2
  5.4 92.4 %factors.1 = (f32[8,9472]{1,0:T(8,128)S(1)}, f32[8,128]{1,0:T(8,128)S(1)}) custom-call(bf16[1,112,9472]{2,1,0:T(8,128)(2,1)S(1)} %copy-done.1, f32[1,112,9472]{2,1,0:T(8,128)S(1)} %copy-done, f32[8,9472]{1,0:T(8,128)S(1)} %copy-done.2), custom_call_target="tpu_custom_call" | custom-call | tf_op jit(solution)/shard_map/factors/pallas_call | solution.py:324
  97.8 5.4 %outputs.1 = (bf16[112,9472]{1,0:T(8,128)(2,1)}, f32[1,112,9472]{2,1,0:T(8,128)}, f32[8,9472]{1,0:T(8,128)}) custom-call(f32[8,128]{1,0:T(8,128)S(1)} %get-tuple-element.5.p, f32[8,9472]{1,0:T(8,128)S(1)} %get-tuple-element.6.q, bf16[1,112,9472]{2,1,0:T(8,128)(2,1)S(1)} %copy-done.1, f32[1,112,9472]{2,1,0:T(8,128)S(1)} %copy-done), custom_call_target="tpu_custom_call" | custom-call | tf_op jit(solution)/shard_map/outputs/pallas_call | solution.py:394
Async XLA Ops:
  0.6 2.2 %copy-start = (f32[1,112,9472]{2,1,0:T(8,128)S(1)}, f32[1,112,9472]{2,1,0:T(8,128)}, u32[]{:S(2)}) copy-start(f32[1,112,9472]{2,1,0:T(8,128)} %error.3) | copy-start | bytes 12730372
  2.8 1.6 %copy-start.1 = (bf16[1,112,9472]{2,1,0:T(8,128)(2,1)S(1)}, bf16[1,112,9472]{2,1,0:T(8,128)(2,1)}, u32[]{:S(2)}) copy-start(bf16[1,112,9472]{2,1,0:T(8,128)(2,1)} %grad.3) | copy-start | bytes 6365188
  4.4 1.0 copy-start.2

commit v2 on v1

--- a/solution.py
+++ b/solution.py
@@ -11,6 +11,7 @@
 RANK = 8
 ROWS = 112
 HALF = 56
+SLOT = 64
 COLS = 9472
 LANE = 128
 WIN = 640
@@ -19,6 +20,10 @@
 PART = 24
 CHUNK = 10 * LANE
 STARTS = tuple(range(0, COLS, CHUNK))
+PLANE = sorted(
+    ((i, j) for i in range(4) for j in range(4) if i or j),
+    key=lambda ij: -(min(ij[0], 4 - ij[0]) + min(ij[1], 4 - ij[1])),
+)
 
 
 def nt(a, b):
@@ -66,10 +71,10 @@
 
 
 def power(
-    grad, error, q_init, q_out, p_out,
-    gbuf, m, qv, cr, ra, rb, fm, fp, sx, s, s_high, s_low,
+    grad, error, q_init, q_out, p_out, m,
+    gbuf, qv, cr, ra, rb, fm, fp, sx, s, s_high, s_low,
     p1s, p1r, qs, cbuf, zs, zbuf, qall, ps, pbuf, pfin, qfin,
-    lsem, csend, crecv, ysend, yrecv, xsem, p1sem, c1sem, zsem, c2sem, psem, fsem,
+    lsem, csend, crecv, ysend, yrecv, xsend, xrecv, p1sem, c1sem, zsem, c2sem, psem, fsem, qsend, qsame, qcross,
 ):
     d, t = lax.axis_index("dp"), lax.axis_index("tensor")
     y, c = d // 2, d % 2
@@ -81,10 +86,10 @@
     other = at(y, 1 - c, x, z)
     ahead_y, behind_y, far_y = (y + 1 + 2 * c) % 4, (y + 3 - 2 * c) % 4, (y + 2) % 4
     ahead, behind = at(ahead_y, c, x, z), at(behind_y, c, x, z)
-    plane = [((y + j) % 4, (x + i) % 4) for i in range(4) for j in range(4)]
-    plane_same = [at(yy, c, xx, z) for yy, xx in plane[1:]]
-    plane_other = [at(yy, 1 - c, xx, z) for yy, xx in plane[1:]]
-    line = [at(y, c, x, (z + k) % 8) for k in range(1, 8)]
+    plane = [((y + j) % 4, (x + i) % 4) for i, j in PLANE]
+    plane_same = [at(yy, c, xx, z) for yy, xx in plane]
+    plane_other = [at(yy, 1 - c, xx, z) for yy, xx in plane]
+    line = [at(y, c, x, (z + k) % 8) for k in (4, 3, 5, 2, 6, 1, 7)]
 
     def remote(src, dst, send, recv, device):
         copy = pltpu.make_async_remote_copy(
@@ -96,7 +101,7 @@
         pltpu.make_async_copy(ref, ref, sem).wait()
 
     barrier = pltpu.get_barrier_semaphore()
-    partners = [other] + plane_same + plane_other + line
+    partners = line + plane_same + plane_other + [other]
     for device in partners:
         pl.semaphore_signal(barrier, inc=1, device_id=device, device_id_type=MESH)
 
@@ -126,23 +131,32 @@
     mine = pl.ds(pl.multiple_of(HALF * c, 8), HALF)
     theirs = pl.ds(pl.multiple_of(HALF * (1 - c), 8), HALF)
     order = [(x + 1 + j) % 4 for j in range(4)]
+    for xx in range(4):
+        s[SLOT * xx + HALF : SLOT * (xx + 1), :] = jnp.zeros((SLOT - HALF, WIN), F32)
+    turn = (far_y, ahead_y, behind_y, y)
+    turn_there = (far_y, behind_y, ahead_y, y)
     for j in range(4):
-        for yy in range(4):
-            remote(m.at[theirs, window(yy, order[j])], cr.at[order[j], yy], csend.at[j], crecv.at[j], other)
+        for k in range(4):
+            yy = turn_there[k]
+            remote(m.at[theirs, window(yy, order[j])], cr.at[order[j], yy], csend.at[j], crecv.at[k, j], other)
 
     top, low = pl.ds(0, TOP), pl.ds(TOP, HALF - TOP)
 
     def first(j):
         xx = order[j]
-        wait(cr.at[xx], crecv.at[j])
-        cr[xx, far_y] = cr[xx, far_y] + m[mine, window(far_y, xx)]
+
+        def add(k):
+            wait(cr.at[xx, turn[k]], crecv.at[k, j])
+            cr[xx, turn[k]] = cr[xx, turn[k]] + m[mine, window(turn[k], xx)]
+
+        add(0)
         remote(cr.at[xx, far_y, top], ra.at[j], ysend.at[0, j], yrecv.at[0, j], ahead)
         remote(cr.at[xx, far_y, low], rb.at[j], ysend.at[1, j], yrecv.at[1, j], behind)
-        cr[xx, ahead_y] = cr[xx, ahead_y] + m[mine, window(ahead_y, xx)]
+        add(1)
         remote(cr.at[xx, ahead_y, low], fm.at[j, low], ysend.at[2, j], yrecv.at[2, j], ahead)
-        cr[xx, behind_y] = cr[xx, behind_y] + m[mine, window(behind_y, xx)]
+        add(2)
         remote(cr.at[xx, behind_y, top], fp.at[j, top], ysend.at[3, j], yrecv.at[3, j], behind)
-        cr[xx, y] = cr[xx, y] + m[mine, window(y, xx)]
+        add(3)
 
     def second(j):
         xx = order[j]
@@ -153,7 +167,7 @@
         rb[j] = rb[j] + cr[xx, behind_y, low]
         remote(rb.at[j], fp.at[j, low], ysend.at[5, j], yrecv.at[5, j], behind)
 
-    here = pl.ds(pl.multiple_of(HALF * x, 8), HALF)
+    here = pl.ds(pl.multiple_of(SLOT * x, 8), HALF)
 
     def third(j):
         xx = order[j]
@@ -164,11 +178,12 @@
         total = (fm[j] + fp[j] + cr[xx, y]) * 0.125
         if j < 3:
             sx[j] = total
-            remote(sx.at[j], s.at[here], xsem.at[0], xsem.at[1], at(y, c, xx, z))
+            remote(sx.at[j], s.at[here], xsend.at[0], xrecv.at[j], at(y, c, xx, z))
         else:
             s[here] = total
 
     first(0)
+    first(1)
 
     q_two = stacked(qv[...])
     p_term = jnp.zeros((RANK, ROWS), F32)
@@ -189,17 +204,13 @@
         remote(p1s.at[1 - c], p1r.at[place], p1sem.at[0], p1sem.at[1], cross)
     remote(p1s.at[1 - c], p1r.at[place], p1sem.at[0], p1sem.at[1], other)
 
-    first(1)
     second(0)
     first(2)
     second(1)
     third(0)
+    second(2)
     first(3)
-    second(2)
     third(1)
-    second(3)
-    third(2)
-    third(3)
 
     wait(p1r.at[pl.ds(0, 31)], p1sem.at[1])
     blocks = []
@@ -207,15 +218,28 @@
         total = p1r[8 * xx]
         for dd in range(1, 8):
             total = total + p1r[8 * xx + dd]
-        blocks.append(total[:, :HALF])
+        blocks.append(total[:, :SLOT])
     p_sum = jnp.concatenate(blocks, axis=1) * 0.125
 
-    wait(s.at[pl.ds(0, 3 * HALF)], xsem.at[1])
+    third(2)
+    second(3)
+
     limit = jnp.where(jnp.logical_and(x == 3, y < 3), 3 * LANE, WIN)
-    inside = lax.broadcasted_iota(jnp.int32, (4 * HALF, WIN), 1) < limit
-    high, rest = two_terms(jnp.where(inside, s[...], 0.0))
-    s_high[...] = high.astype(BF16)
-    s_low[...] = rest.astype(BF16)
+    inside = lax.broadcasted_iota(jnp.int32, (SLOT, WIN), 1) < limit
+
+    def terms(xx):
+        rows = pl.ds(pl.multiple_of(SLOT * xx, SLOT), SLOT)
+        high, rest = two_terms(jnp.where(inside, s[rows], 0.0))
+        s_high[rows] = high.astype(BF16)
+        s_low[rows] = rest.astype(BF16)
+
+    for j in range(2):
+        wait(sx.at[j], xrecv.at[j])
+        terms((x + 3 - j) % 4)
+    third(3)
+    terms(x)
+    wait(sx.at[2], xrecv.at[2])
+    terms((x + 1) % 4)
 
     own = pl.ds(pl.multiple_of(PART * c, 8), PART)
     cross = pl.ds(pl.multiple_of(PART * (1 - c), 8), PART)
@@ -238,10 +262,10 @@
             qs[i, PART * half + 20 : PART * half + 24, :] = gram[ranks]
         remote(qs.at[i, cross], cbuf.at[i], c1sem.at[0, i], c1sem.at[1, i], other)
         if last:
-            rows = jnp.zeros((RANK, HALF), F32)
+            rows = jnp.zeros((RANK, SLOT), F32)
             for xx in range(4):
-                rows = jnp.where(x == xx, p_sum[:, HALF * xx : HALF * xx + HALF], rows)
-            pfin[c] = jnp.concatenate([rows, blank], axis=1)
+                rows = jnp.where(x == xx, p_sum[:, SLOT * xx : SLOT * (xx + 1)], rows)
+            pfin[c] = jnp.concatenate([rows, jnp.zeros((RANK, LANE - SLOT), F32)], axis=1)
             remote(pfin.at[c], pfin.at[c], fsem.at[0], fsem.at[1], other)
         wait(cbuf.at[i], c1sem.at[1, i])
         zs[i] = qs[i, own] + cbuf[i]
@@ -262,9 +286,7 @@
         a, b = nt(q_two, s_high[...]), nt(q_two, s_low[...])
         p_raw = (a[:RANK] + a[RANK:]) + (b[:RANK] + b[RANK:])
         ps[i, 0:RANK, :] = p_raw[:, :LANE]
-        ps[i, RANK : 2 * RANK, :] = jnp.concatenate(
-            [p_raw[:, LANE:], jnp.zeros((RANK, 2 * LANE - 4 * HALF), F32)], axis=1
-        )
+        ps[i, RANK : 2 * RANK, :] = p_raw[:, LANE:]
         for device in plane_same:
             remote(ps.at[i], pbuf.at[i, me], psem.at[0, i], psem.at[1, i], device)
         pbuf[i, me] = ps[i]
@@ -273,29 +295,45 @@
         p_raw = pbuf[i, 0]
         for k in range(1, 16):
             p_raw = p_raw + pbuf[i, k]
-        p_raw = jnp.concatenate([p_raw[:RANK], p_raw[RANK:, : 4 * HALF - LANE]], axis=1)
+        p_raw = jnp.concatenate([p_raw[:RANK], p_raw[RANK:]], axis=1)
         p_sum = apply(inverse, p_raw)
 
     slot = me * 2 + c
     qfin[slot] = total
-    remote(qfin.at[slot], qfin.at[slot], fsem.at[2], fsem.at[3], other)
-    for same, cross in zip(plane_same, plane_other):
-        remote(qfin.at[slot], qfin.at[slot], fsem.at[4], fsem.at[5], same)
-        remote(qfin.at[slot], qfin.at[slot], fsem.at[4], fsem.at[5], cross)
-    wait(qfin.at[slot], fsem.at[3])
+    remote(qfin.at[slot], qfin.at[slot], qsend.at[1], qcross.at[me], other)
+    for device in plane_same:
+        remote(qfin.at[slot], qfin.at[slot], qsend.at[0], qsame.at[me], device)
+    wait(qfin.at[0], qcross.at[me])
     wait(pfin.at[c], fsem.at[1])
     _, gram = by_column(qfin[me * 2], qfin[me * 2 + 1])
     inverse = inverse_factor(gram)
     p_hat = apply(inverse, jnp.concatenate([pfin[0][:, :HALF], pfin[1][:, :HALF]], axis=1))
     p_out[...] = jnp.concatenate([p_hat, jnp.zeros((RANK, LANE - ROWS), F32)], axis=1)
-    wait(qfin.at[pl.ds(0, 30)], fsem.at[5])
-    for yy in range(4):
-        for xx in range(4):
-            group = (yy * 4 + xx) * 2
-            q_raw, _ = by_column(qfin[group], qfin[group + 1])
-            width = 3 * LANE if xx == 3 and yy < 3 else WIN
-            start = yy * STEP_Y + xx * WIN
-            q_out[:, start : start + width] = apply(inverse, q_raw[:, :width])
+
+    def result(yy, xx, arrived=False):
+        group = yy * 4 + xx
+        if not arrived:
+            wait(qfin.at[0], qcross.at[group])
+        q_raw, _ = by_column(qfin[group * 2], qfin[group * 2 + 1])
+        q_sum = apply(inverse, q_raw)
+        start = pl.multiple_of(yy * STEP_Y + xx * WIN, LANE)
+        q_out[:, pl.ds(start, 3 * LANE)] = q_sum[:, : 3 * LANE]
+
+        @pl.when(jnp.logical_or(xx < 3, yy == 3))
+        def _():
+            q_out[:, pl.ds(pl.multiple_of(start + 3 * LANE, LANE), 2 * LANE)] = q_sum[:, 3 * LANE :]
+
+    result(y, x, True)
+    nearest = plane[::-1]
+    for k, (yy, xx) in enumerate(nearest):
+        group = yy * 4 + xx
+        wait(qfin.at[0], qsame.at[group])
+        passed = qfin.at[group * 2 + c]
+        remote(passed, passed, qsend.at[1], qcross.at[group], other)
+        if k > 1:
+            result(*nearest[k - 2])
+    result(*nearest[-2])
+    result(*nearest[-1])
 
     for j in range(4):
         wait(cr.at[j], csend.at[j])
@@ -305,7 +343,7 @@
         wait(fp.at[j, top], ysend.at[3, j])
         wait(ra.at[j], ysend.at[4, j])
         wait(rb.at[j], ysend.at[5, j])
-    wait(sx, xsem.at[0])
+    wait(sx, xsend.at[0])
     wait(p1r.at[pl.ds(0, 31)], p1sem.at[0])
     for i in range(ITERS):
         wait(cbuf.at[i], c1sem.at[0, i])
@@ -314,8 +352,8 @@
             wait(cbuf.at[i], c2sem.at[0, i])
             wait(pbuf.at[i, pl.ds(0, 15)], psem.at[0, i])
     wait(pfin.at[0], fsem.at[0])
-    wait(cbuf.at[0], fsem.at[2])
-    wait(qfin.at[pl.ds(0, 30)], fsem.at[4])
+    wait(qfin.at[pl.ds(0, 15)], qsend.at[0])
+    wait(qfin.at[pl.ds(0, 16)], qsend.at[1])
 
 
 def factors(grad, error, q_init):
@@ -327,12 +365,12 @@
         out_shape=(
             jax.ShapeDtypeStruct((RANK, COLS), F32),
             jax.ShapeDtypeStruct((RANK, LANE), F32),
+            jax.ShapeDtypeStruct((ROWS, COLS), F32),
         ),
-        in_specs=[pl.BlockSpec(memory_space=pl.ANY)] * 3,
-        out_specs=(pl.BlockSpec(memory_space=vmem), pl.BlockSpec(memory_space=vmem)),
+        in_specs=[pl.BlockSpec(memory_space=pltpu.HBM)] * 3,
+        out_specs=(pl.BlockSpec(memory_space=vmem),) * 3,
         scratch_shapes=[
             vmem((ROWS, COLS), BF16),
-            vmem((ROWS, COLS), F32),
             vmem((RANK, COLS), F32),
             vmem((4, 4, HALF, WIN), F32),
             vmem((4, TOP, WIN), F32),
@@ -340,9 +378,9 @@
             vmem((4, HALF, WIN), F32),
             vmem((4, HALF, WIN), F32),
             vmem((3, HALF, WIN), F32),
-            vmem((4 * HALF, WIN), F32),
-            vmem((4 * HALF, WIN), BF16),
-            vmem((4 * HALF, WIN), BF16),
+            vmem((4 * SLOT, WIN), F32),
+            vmem((4 * SLOT, WIN), BF16),
+            vmem((4 * SLOT, WIN), BF16),
             vmem((2, RANK, LANE), F32),
             vmem((32, RANK, LANE), F32),
             vmem((ITERS, 2 * PART, LANE), F32),
@@ -356,59 +394,72 @@
             vmem((32, PART, LANE), F32),
             dma((2 * len(STARTS) + 1,)),
             dma((4,)),
-            dma((4,)),
+            dma((4, 4)),
             dma((6, 4)),
             dma((6, 4)),
-            dma((2,)),
+            dma((1,)),
+            dma((3,)),
             dma((2,)),
             dma((2, ITERS)),
             dma((2, ITERS)),
             dma((2, ITERS)),
             dma((2, ITERS)),
-            dma((6,)),
+            dma((2,)),
+            dma((2,)),
+            dma((16,)),
+            dma((16,)),
         ],
         compiler_params=pltpu.CompilerParams(
             collective_id=0, has_side_effects=True, vmem_limit_bytes=40 * 2**20
         ),
-    )(grad, error, q_init)
-
-
-def finish(p, q, grad, error, decompressed, new_error, q_next):
+    )(*(pltpu.with_memory_space_constraint(a, pltpu.HBM) for a in (grad, error, q_init)))
+
+
+def finish(p, q, m, decompressed, new_error, q_next, dbuf, ebuf, sem):
+    copies = [pltpu.make_async_copy(q, q_next, sem.at[0])]
+    copies[0].start()
     p_high, p_rest = two_terms(p[:, :ROWS])
-    q_high, q_rest = two_terms(q[...])
     left = jnp.concatenate([p_high, p_high, p_rest, p_rest], axis=0).astype(BF16)
-    right = jnp.concatenate([q_high, q_rest, q_high, q_rest], axis=0).astype(BF16)
-    approx = lax.dot_general(
-        left, right, (((0,), (0,)), ((), ())), preferred_element_type=F32
-    )
-    decompressed[...] = approx.astype(BF16)
-    new_error[...] = (grad[...].astype(F32) + error[...]) - approx
-    q_next[...] = q[...]
-
-
-def outputs(p_hat, q_sum, grad, error):
-    def block(rows):
-        return pl.BlockSpec((rows, CHUNK), lambda i: (0, i))
-
-    whole = pl.BlockSpec((None, ROWS, CHUNK), lambda i: (0, 0, i))
+    for i, start in enumerate(STARTS):
+        columns = pl.ds(start, min(CHUNK, COLS - start))
+        q_high, q_rest = two_terms(q[:, columns])
+        right = jnp.concatenate([q_high, q_rest, q_high, q_rest], axis=0).astype(BF16)
+        approx = lax.dot_general(
+            left, right, (((0,), (0,)), ((), ())), preferred_element_type=F32
+        )
+        ebuf[:, columns] = m[:, columns] - approx
+        copies.append(pltpu.make_async_copy(ebuf.at[:, columns], new_error.at[0, :, columns], sem.at[2 * i + 1]))
+        copies[-1].start()
+        dbuf[:, columns] = approx.astype(BF16)
+        copies.append(pltpu.make_async_copy(dbuf.at[:, columns], decompressed.at[:, columns], sem.at[2 * i + 2]))
+        copies[-1].start()
+    for copy in copies:
+        copy.wait()
+
+
+def outputs(p_hat, q_sum, merged):
     return pl.pallas_call(
         finish,
         name="outputs",
-        grid=(len(STARTS),),
-        in_specs=[pl.BlockSpec((RANK, LANE), lambda i: (0, 0)), block(RANK), whole, whole],
-        out_specs=(block(ROWS), whole, block(RANK)),
+        in_specs=[pl.BlockSpec(memory_space=pltpu.VMEM)] * 3,
+        out_specs=(pl.BlockSpec(memory_space=pltpu.HBM),) * 3,
         out_shape=(
             jax.ShapeDtypeStruct((ROWS, COLS), BF16),
             jax.ShapeDtypeStruct((1, ROWS, COLS), F32),
             jax.ShapeDtypeStruct((RANK, COLS), F32),
         ),
+        scratch_shapes=[
+            pltpu.VMEM((ROWS, COLS), BF16),
+            pltpu.VMEM((ROWS, COLS), F32),
+            pltpu.SemaphoreType.DMA((2 * len(STARTS) + 1,)),
+        ],
         compiler_params=pltpu.CompilerParams(vmem_limit_bytes=24 * 2**20),
-    )(p_hat, q_sum, grad, error)
+    )(p_hat, q_sum, merged)
 
 
 def local(grad, error, q_init):
-    q_sum, p_hat = factors(grad, error, q_init)
-    return outputs(p_hat, q_sum, grad, error)
+    q_sum, p_hat, merged = factors(grad, error, q_init)
+    return outputs(p_hat, q_sum, merged)
 
 
 def solution(mesh):

time: 103 us -> 93.3 us (0.906)
  Pallas kernels: 97.8 us -> 92.6 us
  local copies, waits for them, and re-layouts: 4.76 us -> 0 us
    unnamed x6 -> x0, local copies, waits for them, and re-layouts: 4.76 us -> none
    pallas_call x1, Pallas kernels: 92.4 us -> 89.6 us  [factors(): pl.pallas_call(power, name='factors', out_shape=(jax.ShapeDtypeStruct((RA...]
    pallas_call x1, Pallas kernels: 5.39 us -> 3.06 us  [outputs(): pl.pallas_call(finish, name='outputs', in_specs=[pl.BlockSpec(memory_spac...]
where the time goes in v2:
time: 93.3 us
  Pallas kernels  92.6 us (99%)
    pallas_call x1, Pallas kernels, factors(): pl.pallas_call(power, name='factors', out_shape=(jax.ShapeDtypeStruct((RA...  89.6 us
    pallas_call x1, Pallas kernels, outputs(): pl.pallas_call(finish, name='outputs', in_specs=[pl.BlockSpec(memory_spac...  3.06 us

profile of v2, /device:TPU:1, one launch (start us, length us, event | category | flops | bytes accessed | tf_op | source)
XLA Modules:
  0.0 93.3 jit_solution(2848228590558542205)
XLA Ops:
  0.6 89.6 %factors.1 = (f32[8,9472]{1,0:T(8,128)S(1)}, f32[8,128]{1,0:T(8,128)S(1)}, f32[112,9472]{1,0:T(8,128)S(1)}) custom-call(bf16[1,112,9472]{2,1,0:T(8,128)(2,1)} %grad.1, f32[1,112,9472]{2,1,0:T(8,128)} %error.1, f32[8,9472]{1,0:T(8,128)} %q_init.1), custom_call_target="tpu_custom_call" | custom-call | tf_op jit(solution)/shard_map/factors/pallas_call | solution.py:362
  90.2 3.1 %outputs.1 = (bf16[112,9472]{1,0:T(8,128)(2,1)}, f32[1,112,9472]{2,1,0:T(8,128)}, f32[8,9472]{1,0:T(8,128)}) custom-call(f32[8,128]{1,0:T(8,128)S(1)} %get-tuple-element.6.p, f32[8,9472]{1,0:T(8,128)S(1)} %get-tuple-element.7.q, f32[112,9472]{1,0:T(8,128)S(1)} %get-tuple-element.8.m), custom_call_target="tpu_custom_call" | custom-call | tf_op jit(solution)/shard_map/outputs/pallas_call | solution.py:441

commit v3 on v2

--- a/solution.py
+++ b/solution.py
@@ -15,7 +15,6 @@
 COLS = 9472
 LANE = 128
 WIN = 640
-STEP_Y = 18 * LANE
 TOP = 32
 PART = 24
 CHUNK = 10 * LANE
@@ -24,6 +23,10 @@
     ((i, j) for i in range(4) for j in range(4) if i or j),
     key=lambda ij: -(min(ij[0], 4 - ij[0]) + min(ij[1], 4 - ij[1])),
 )
+
+
+def first_tile(y, x):
+    return 18 * y + y // 2 + 5 * x
 
 
 def nt(a, b):
@@ -73,9 +76,10 @@
 def power(
     grad, error, q_init, q_out, p_out, m,
     gbuf, qv, cr, ra, rb, fm, fp, sx, s, s_high, s_low,
-    p1s, p1r, qs, cbuf, zs, zbuf, qall, ps, pbuf, pfin, qfin,
+    p1y, p1x, qs, cbuf, zs, zbuf, qall, ps, pbuf, pfin, qfin,
     lsem, csend, crecv, ysend, yrecv, xsend, xrecv, p1sem, c1sem, zsem, c2sem, psem, fsem, qsend, qsame, qcross,
 ):
+    s[...] = jnp.zeros_like(s)
     d, t = lax.axis_index("dp"), lax.axis_index("tensor")
     y, c = d // 2, d % 2
     x, z = t // 8, t % 8
@@ -125,106 +129,139 @@
     q_load.wait()
     pl.semaphore_wait(barrier, len(partners))
 
-    def window(yy, xx):
-        return pl.ds(pl.multiple_of(yy * STEP_Y + xx * WIN, LANE), WIN)
+    def window(yy, xx, width):
+        return pl.ds(pl.multiple_of(first_tile(yy, xx) * LANE, LANE), width)
+
+    def sized(xx, body):
+        @pl.when(xx < 3)
+        def _():
+            body(WIN)
+
+        @pl.when(xx == 3)
+        def _():
+            body(WIN - LANE)
 
     mine = pl.ds(pl.multiple_of(HALF * c, 8), HALF)
     theirs = pl.ds(pl.multiple_of(HALF * (1 - c), 8), HALF)
     order = [(x + 1 + j) % 4 for j in range(4)]
-    for xx in range(4):
-        s[SLOT * xx + HALF : SLOT * (xx + 1), :] = jnp.zeros((SLOT - HALF, WIN), F32)
     turn = (far_y, ahead_y, behind_y, y)
     turn_there = (far_y, behind_y, ahead_y, y)
+    top, low = pl.ds(0, TOP), pl.ds(TOP, HALF - TOP)
+    here = pl.ds(pl.multiple_of(SLOT * x, 8), HALF)
+
+    def cross_core(j):
+        def body(width):
+            for k in range(4):
+                yy = turn_there[k]
+                remote(
+                    m.at[theirs, window(yy, order[j], width)],
+                    cr.at[order[j], yy, :, pl.ds(0, width)],
+                    csend.at[j], crecv.at[k, j], other,
+                )
+
+        sized(order[j], body)
+
+    def add(j, k, width):
+        columns = pl.ds(0, width)
+        place = cr.at[order[j], turn[k], :, columns]
+        wait(place, crecv.at[k, j])
+        place[...] = place[...] + m[mine, window(turn[k], order[j], width)]
+
+    def first(j, added=False):
+        def body(width):
+            columns = pl.ds(0, width)
+            xx = order[j]
+            if not added:
+                add(j, 0, width)
+            remote(cr.at[xx, far_y, top, columns], ra.at[j, :, columns], ysend.at[0, j], yrecv.at[0, j], ahead)
+            remote(cr.at[xx, far_y, low, columns], rb.at[j, :, columns], ysend.at[1, j], yrecv.at[1, j], behind)
+            if not added:
+                add(j, 1, width)
+            remote(cr.at[xx, ahead_y, low, columns], fm.at[j, low, columns], ysend.at[2, j], yrecv.at[2, j], ahead)
+            if not added:
+                add(j, 2, width)
+            remote(cr.at[xx, behind_y, top, columns], fp.at[j, top, columns], ysend.at[3, j], yrecv.at[3, j], behind)
+            if not added:
+                add(j, 3, width)
+
+        sized(order[j], body)
+
+    def only_add(j):
+        def body(width):
+            for k in range(4):
+                add(j, k, width)
+
+        sized(order[j], body)
+
+    def second(j):
+        def body(width):
+            columns = pl.ds(0, width)
+            xx = order[j]
+            a, b = ra.at[j, :, columns], rb.at[j, :, columns]
+            wait(a, yrecv.at[0, j])
+            a[...] = a[...] + cr[xx, ahead_y, top, columns]
+            remote(a, fm.at[j, top, columns], ysend.at[4, j], yrecv.at[4, j], ahead)
+            wait(b, yrecv.at[1, j])
+            b[...] = b[...] + cr[xx, behind_y, low, columns]
+            remote(b, fp.at[j, low, columns], ysend.at[5, j], yrecv.at[5, j], behind)
+
+        sized(order[j], body)
+
+    def third(j):
+        def body(width):
+            columns = pl.ds(0, width)
+            xx = order[j]
+            wait(fm.at[j, low, columns], yrecv.at[2, j])
+            wait(fp.at[j, top, columns], yrecv.at[3, j])
+            wait(fm.at[j, top, columns], yrecv.at[4, j])
+            wait(fp.at[j, low, columns], yrecv.at[5, j])
+            total = (fm[j, :, columns] + fp[j, :, columns] + cr[xx, y, :, columns]) * 0.125
+            if j < 3:
+                sx[j, :, columns] = total
+                remote(sx.at[j, :, columns], s.at[here, columns], xsend.at[j], xrecv.at[j], at(y, c, xx, z))
+            else:
+                s[here, columns] = total
+
+        sized(order[j], body)
+
     for j in range(4):
-        for k in range(4):
-            yy = turn_there[k]
-            remote(m.at[theirs, window(yy, order[j])], cr.at[order[j], yy], csend.at[j], crecv.at[k, j], other)
-
-    top, low = pl.ds(0, TOP), pl.ds(TOP, HALF - TOP)
-
-    def first(j):
-        xx = order[j]
-
-        def add(k):
-            wait(cr.at[xx, turn[k]], crecv.at[k, j])
-            cr[xx, turn[k]] = cr[xx, turn[k]] + m[mine, window(turn[k], xx)]
-
-        add(0)
-        remote(cr.at[xx, far_y, top], ra.at[j], ysend.at[0, j], yrecv.at[0, j], ahead)
-        remote(cr.at[xx, far_y, low], rb.at[j], ysend.at[1, j], yrecv.at[1, j], behind)
-        add(1)
-        remote(cr.at[xx, ahead_y, low], fm.at[j, low], ysend.at[2, j], yrecv.at[2, j], ahead)
-        add(2)
-        remote(cr.at[xx, behind_y, top], fp.at[j, top], ysend.at[3, j], yrecv.at[3, j], behind)
-        add(3)
-
-    def second(j):
-        xx = order[j]
-        wait(ra.at[j], yrecv.at[0, j])
-        ra[j] = ra[j] + cr[xx, ahead_y, top]
-        remote(ra.at[j], fm.at[j, top], ysend.at[4, j], yrecv.at[4, j], ahead)
-        wait(rb.at[j], yrecv.at[1, j])
-        rb[j] = rb[j] + cr[xx, behind_y, low]
-        remote(rb.at[j], fp.at[j, low], ysend.at[5, j], yrecv.at[5, j], behind)
-
-    here = pl.ds(pl.multiple_of(SLOT * x, 8), HALF)
-
-    def third(j):
-        xx = order[j]
-        wait(fm.at[j, low], yrecv.at[2, j])
-        wait(fp.at[j, top], yrecv.at[3, j])
-        wait(fm.at[j, top], yrecv.at[4, j])
-        wait(fp.at[j, low], yrecv.at[5, j])
-        total = (fm[j] + fp[j] + cr[xx, y]) * 0.125
-        if j < 3:
-            sx[j] = total
-            remote(sx.at[j], s.at[here], xsend.at[0], xrecv.at[j], at(y, c, xx, z))
-        else:
-            s[here] = total
-
+        cross_core(j)
     first(0)
     first(1)
+    first(2)
+    only_add(3)
 
     q_two = stacked(qv[...])
-    p_term = jnp.zeros((RANK, ROWS), F32)
-    for start in STARTS:
-        stop = min(start + CHUNK, COLS)
-        high, rest = two_terms(m[:, start:stop])
-        q_part = q_two[:, start:stop]
-        on_high = nt(q_part, high.astype(BF16))
-        on_rest = nt(q_part, rest.astype(BF16))
-        p_term = p_term + (on_high[:RANK] + on_high[RANK:]) + (on_rest[:RANK] + on_rest[RANK:])
-    blank = jnp.zeros((RANK, LANE - HALF), F32)
-    for half in range(2):
-        p1s[half] = jnp.concatenate([p_term[:, HALF * half : HALF * half + HALF], blank], axis=1)
-    place = x * 8 + d
-    p1r[place] = p1s[c]
-    for same, cross in zip(plane_same, plane_other):
-        remote(p1s.at[c], p1r.at[place], p1sem.at[0], p1sem.at[1], same)
-        remote(p1s.at[1 - c], p1r.at[place], p1sem.at[0], p1sem.at[1], cross)
-    remote(p1s.at[1 - c], p1r.at[place], p1sem.at[0], p1sem.at[1], other)
+    p_term = jnp.zeros((RANK, HALF), F32)
+    for yy in range(4):
+        for xx in range(4):
+            start = first_tile(yy, xx) * LANE
+            width = (5 if xx < 3 else 3 + yy % 2) * LANE
+            high, rest = two_terms(cr[xx, yy, :, :width])
+            q_part = q_two[:, start : start + width]
+            on_high = nt(q_part, high.astype(BF16))
+            on_rest = nt(q_part, rest.astype(BF16))
+            p_term = p_term + (on_high[:RANK] + on_high[RANK:]) + (on_rest[:RANK] + on_rest[RANK:])
+    p1y[y] = jnp.concatenate([p_term, jnp.zeros((RANK, LANE - HALF), F32)], axis=1)
+    for k in (2, 1, 3):
+        remote(p1y.at[y], p1y.at[y], p1sem.at[0], p1sem.at[1], at((y + k) % 4, c, x, z))
 
     second(0)
-    first(2)
     second(1)
+    wait(p1y.at[pl.ds(0, 3)], p1sem.at[1])
+    p1x[x] = ((p1y[0] + p1y[1]) + (p1y[2] + p1y[3])) * 0.125
+    for k in (2, 1, 3):
+        remote(p1x.at[x], p1x.at[x], p1sem.at[2], p1sem.at[3], at(y, c, (x + k) % 4, z))
     third(0)
     second(2)
-    first(3)
+    first(3, True)
     third(1)
-
-    wait(p1r.at[pl.ds(0, 31)], p1sem.at[1])
-    blocks = []
-    for xx in range(4):
-        total = p1r[8 * xx]
-        for dd in range(1, 8):
-            total = total + p1r[8 * xx + dd]
-        blocks.append(total[:, :SLOT])
-    p_sum = jnp.concatenate(blocks, axis=1) * 0.125
-
+    wait(p1x.at[pl.ds(0, 3)], p1sem.at[3])
+    p_sum = jnp.concatenate([p1x[xx][:, :SLOT] for xx in range(4)], axis=1)
     third(2)
     second(3)
 
-    limit = jnp.where(jnp.logical_and(x == 3, y < 3), 3 * LANE, WIN)
+    limit = jnp.where(x == 3, (3 + y % 2) * LANE, WIN)
     inside = lax.broadcasted_iota(jnp.int32, (SLOT, WIN), 1) < limit
 
     def terms(xx):
@@ -233,13 +270,15 @@
         s_high[rows] = high.astype(BF16)
         s_low[rows] = rest.astype(BF16)
 
-    for j in range(2):
-        wait(sx.at[j], xrecv.at[j])
+    def from_x(j):
+        sized(x, lambda width: wait(sx.at[j, :, pl.ds(0, width)], xrecv.at[j]))
         terms((x + 3 - j) % 4)
+
+    from_x(0)
+    from_x(1)
     third(3)
     terms(x)
-    wait(sx.at[2], xrecv.at[2])
-    terms((x + 1) % 4)
+    from_x(2)
 
     own = pl.ds(pl.multiple_of(PART * c, 8), PART)
     cross = pl.ds(pl.multiple_of(PART * (1 - c), 8), PART)
@@ -310,41 +349,47 @@
     p_hat = apply(inverse, jnp.concatenate([pfin[0][:, :HALF], pfin[1][:, :HALF]], axis=1))
     p_out[...] = jnp.concatenate([p_hat, jnp.zeros((RANK, LANE - ROWS), F32)], axis=1)
 
-    def result(yy, xx, arrived=False):
-        group = yy * 4 + xx
-        if not arrived:
-            wait(qfin.at[0], qcross.at[group])
-        q_raw, _ = by_column(qfin[group * 2], qfin[group * 2 + 1])
-        q_sum = apply(inverse, q_raw)
-        start = pl.multiple_of(yy * STEP_Y + xx * WIN, LANE)
-        q_out[:, pl.ds(start, 3 * LANE)] = q_sum[:, : 3 * LANE]
-
-        @pl.when(jnp.logical_or(xx < 3, yy == 3))
-        def _():
-            q_out[:, pl.ds(pl.multiple_of(start + 3 * LANE, LANE), 2 * LANE)] = q_sum[:, 3 * LANE :]
-
-    result(y, x, True)
     nearest = plane[::-1]
-    for k, (yy, xx) in enumerate(nearest):
+    for yy, xx in nearest:
         group = yy * 4 + xx
         wait(qfin.at[0], qsame.at[group])
         passed = qfin.at[group * 2 + c]
         remote(passed, passed, qsend.at[1], qcross.at[group], other)
-        if k > 1:
-            result(*nearest[k - 2])
-    result(*nearest[-2])
-    result(*nearest[-1])
+    by_rank = [jnp.broadcast_to(inverse[:, j : j + 1], (RANK, LANE)) for j in range(RANK)]
+    for yy, xx in nearest:
+        wait(qfin.at[0], qcross.at[yy * 4 + xx])
+    for yy in range(4):
+        for xx in range(4):
+            group, start = yy * 4 + xx, first_tile(yy, xx)
+            for k in range(5 if xx < 3 else 3 + yy % 2):
+                terms_of = [
+                    by_rank[j] * qfin[2 * group + j // 4, 4 * k + j % 4 : 4 * k + j % 4 + 1, :]
+                    for j in range(RANK)
+                ]
+                tile = ((terms_of[0] + terms_of[1]) + (terms_of[2] + terms_of[3])) + (
+                    (terms_of[4] + terms_of[5]) + (terms_of[6] + terms_of[7])
+                )
+                q_out[:, LANE * (start + k) : LANE * (start + k + 1)] = tile
+
+    def left(j):
+        def body(width):
+            columns = pl.ds(0, width)
+            wait(cr.at[order[j], :, :, columns], csend.at[j])
+            wait(ra.at[j, :, columns], ysend.at[0, j])
+            wait(rb.at[j, :, columns], ysend.at[1, j])
+            wait(fm.at[j, low, columns], ysend.at[2, j])
+            wait(fp.at[j, top, columns], ysend.at[3, j])
+            wait(ra.at[j, :, columns], ysend.at[4, j])
+            wait(rb.at[j, :, columns], ysend.at[5, j])
+            if j < 3:
+                wait(sx.at[j, :, columns], xsend.at[j])
+
+        sized(order[j], body)
 
     for j in range(4):
-        wait(cr.at[j], csend.at[j])
-        wait(ra.at[j], ysend.at[0, j])
-        wait(rb.at[j], ysend.at[1, j])
-        wait(fm.at[j, low], ysend.at[2, j])
-        wait(fp.at[j, top], ysend.at[3, j])
-        wait(ra.at[j], ysend.at[4, j])
-        wait(rb.at[j], ysend.at[5, j])
-    wait(sx, xsend.at[0])
-    wait(p1r.at[pl.ds(0, 31)], p1sem.at[0])
+        left(j)
+    wait(p1y.at[pl.ds(0, 3)], p1sem.at[0])
+    wait(p1x.at[pl.ds(0, 3)], p1sem.at[2])
     for i in range(ITERS):
         wait(cbuf.at[i], c1sem.at[0, i])
         wait(zbuf.at[i, pl.ds(0, 7)], zsem.at[0, i])
@@ -381,8 +426,8 @@
             vmem((4 * SLOT, WIN), F32),
             vmem((4 * SLOT, WIN), BF16),
             vmem((4 * SLOT, WIN), BF16),
-            vmem((2, RANK, LANE), F32),
-            vmem((32, RANK, LANE), F32),
+            vmem((4, RANK, LANE), F32),
+            vmem((4, RANK, LANE), F32),
             vmem((ITERS, 2 * PART, LANE), F32),
             vmem((ITERS, PART, LANE), F32),
             vmem((ITERS, PART, LANE), F32),
@@ -397,9 +442,9 @@
             dma((4, 4)),
             dma((6, 4)),
             dma((6, 4)),
-            dma((1,)),
             dma((3,)),
-            dma((2,)),
+            dma((3,)),
+            dma((4,)),
             dma((2, ITERS)),
             dma((2, ITERS)),
             dma((2, ITERS)),
@@ -415,13 +460,18 @@
     )(*(pltpu.with_memory_space_constraint(a, pltpu.HBM) for a in (grad, error, q_init)))
 
 
+PARTS = (2, 4, 8, 10, 10, 10, 10, 10, 6, 4)
+
+
 def finish(p, q, m, decompressed, new_error, q_next, dbuf, ebuf, sem):
     copies = [pltpu.make_async_copy(q, q_next, sem.at[0])]
     copies[0].start()
     p_high, p_rest = two_terms(p[:, :ROWS])
     left = jnp.concatenate([p_high, p_high, p_rest, p_rest], axis=0).astype(BF16)
-    for i, start in enumerate(STARTS):
-        columns = pl.ds(start, min(CHUNK, COLS - start))
+    start = 0
+    for i, part in enumerate(PARTS):
+        columns = pl.ds(start, part * LANE)
+        start += part * LANE
         q_high, q_rest = two_terms(q[:, columns])
         right = jnp.concatenate([q_high, q_rest, q_high, q_rest], axis=0).astype(BF16)
         approx = lax.dot_general(
@@ -451,7 +501,7 @@
         scratch_shapes=[
             pltpu.VMEM((ROWS, COLS), BF16),
             pltpu.VMEM((ROWS, COLS), F32),
-            pltpu.SemaphoreType.DMA((2 * len(STARTS) + 1,)),
+            pltpu.SemaphoreType.DMA((2 * len(PARTS) + 1,)),
         ],
         compiler_params=pltpu.CompilerParams(vmem_limit_bytes=24 * 2**20),
     )(p_hat, q_sum, merged)

time: 93.3 us -> 89.7 us (0.961)
  Pallas kernels: 92.6 us -> 89 us
    pallas_call x1, Pallas kernels: 89.6 us -> 85.9 us  [factors(): pl.pallas_call(power, name='factors', out_shape=(jax.ShapeDtypeStruct((RA...]
where the time goes in v3:
time: 89.7 us; the launch traced here: 89.6 us
  Pallas kernels  89 us (99%)
    pallas_call x1, Pallas kernels, factors(): pl.pallas_call(power, name='factors', out_shape=(jax.ShapeDtypeStruct((RA...  85.9 us
    pallas_call x1, Pallas kernels, outputs(): pl.pallas_call(finish, name='outputs', in_specs=[pl.BlockSpec(memory_spac...  3.04 us

profile of v3, /device:TPU:1, one launch (start us, length us, event | category | flops | bytes accessed | tf_op | source)
XLA Modules:
  0.0 89.6 jit_solution(8928443834818608896)
XLA Ops:
  0.6 85.9 %factors.1 = (f32[8,9472]{1,0:T(8,128)S(1)}, f32[8,128]{1,0:T(8,128)S(1)}, f32[112,9472]{1,0:T(8,128)S(1)}) custom-call(bf16[1,112,9472]{2,1,0:T(8,128)(2,1)} %grad.1, f32[1,112,9472]{2,1,0:T(8,128)} %error.1, f32[8,9472]{1,0:T(8,128)} %q_init.1), custom_call_target="tpu_custom_call" | custom-call | tf_op jit(solution)/shard_map/factors/pallas_call | solution.py:407
  86.6 3.0 %outputs.1 = (bf16[112,9472]{1,0:T(8,128)(2,1)}, f32[1,112,9472]{2,1,0:T(8,128)}, f32[8,9472]{1,0:T(8,128)}) custom-call(f32[8,128]{1,0:T(8,128)S(1)} %get-tuple-element.6.p, f32[8,9472]{1,0:T(8,128)S(1)} %get-tuple-element.7.q, f32[112,9472]{1,0:T(8,128)S(1)} %get-tuple-element.8.m), custom_call_target="tpu_custom_call" | custom-call | tf_op jit(solution)/shard_map/outputs/pallas_call | solution.py:491

commit v4 on v3

--- a/solution.py
+++ b/solution.py
@@ -92,7 +92,6 @@
     ahead, behind = at(ahead_y, c, x, z), at(behind_y, c, x, z)
     plane = [((y + j) % 4, (x + i) % 4) for i, j in PLANE]
     plane_same = [at(yy, c, xx, z) for yy, xx in plane]
-    plane_other = [at(yy, 1 - c, xx, z) for yy, xx in plane]
     line = [at(y, c, x, (z + k) % 8) for k in (4, 3, 5, 2, 6, 1, 7)]
 
     def remote(src, dst, send, recv, device):
@@ -105,7 +104,7 @@
         pltpu.make_async_copy(ref, ref, sem).wait()
 
     barrier = pltpu.get_barrier_semaphore()
-    partners = line + plane_same + plane_other + [other]
+    partners = line + plane_same + [other]
     for device in partners:
         pl.semaphore_signal(barrier, inc=1, device_id=device, device_id_type=MESH)
 

time: 89.7 us -> 88.3 us (0.984)
  Pallas kernels: 89 us -> 87.6 us
    pallas_call x1, Pallas kernels: 85.9 us -> 84.5 us  [factors(): pl.pallas_call(power, name='factors', out_shape=(jax.ShapeDtypeStruct((RA...]
where the time goes in v4:
time: 88.3 us; the launch traced here: 88.2 us
  Pallas kernels  87.6 us (99%)
    pallas_call x1, Pallas kernels, factors(): pl.pallas_call(power, name='factors', out_shape=(jax.ShapeDtypeStruct((RA...  84.5 us
    pallas_call x1, Pallas kernels, outputs(): pl.pallas_call(finish, name='outputs', in_specs=[pl.BlockSpec(memory_spac...  3.04 us

profile of v4, /device:TPU:1, one launch (start us, length us, event | category | flops | bytes accessed | tf_op | source)
XLA Modules:
  0.0 88.2 jit_solution(17359744593227722017)
XLA Ops:
  0.6 84.5 %factors.1 = (f32[8,9472]{1,0:T(8,128)S(1)}, f32[8,128]{1,0:T(8,128)S(1)}, f32[112,9472]{1,0:T(8,128)S(1)}) custom-call(bf16[1,112,9472]{2,1,0:T(8,128)(2,1)} %grad.1, f32[1,112,9472]{2,1,0:T(8,128)} %error.1, f32[8,9472]{1,0:T(8,128)} %q_init.1), custom_call_target="tpu_custom_call" | custom-call | tf_op jit(solution)/shard_map/factors/pallas_call | solution.py:406
  85.2 3.0 %outputs.1 = (bf16[112,9472]{1,0:T(8,128)(2,1)}, f32[1,112,9472]{2,1,0:T(8,128)}, f32[8,9472]{1,0:T(8,128)}) custom-call(f32[8,128]{1,0:T(8,128)S(1)} %get-tuple-element.6.p, f32[8,9472]{1,0:T(8,128)S(1)} %get-tuple-element.7.q, f32[112,9472]{1,0:T(8,128)S(1)} %get-tuple-element.8.m), custom_call_target="tpu_custom_call" | custom-call | tf_op jit(solution)/shard_map/outputs/pallas_call | solution.py:490
